TPU v7x, 512 devices: a whole 4x8x8 slice. The times are simulated.
512 devices in a mesh: row: 16 (over y, x_hi), col: 2 (over core), depth: 16 (over z, x_lo).
Axes of the slice: x: 4 (x_hi: 2, x_lo: 2; x = x_hi * 2 + x_lo), y: 8, z: 8, core: 2. Of those that a mesh axis runs over, the one named last changes fastest.
Arguments:
- y_blocks: float32 [4096, 4096], P('row', 'col'), may hold values from -6 to 6
- z_blocks: float32 [4096, 4096], P('row', 'col'), may hold values from -0.125 to 0.125
- h_blocks: float32 [4096, 4096], P('row', 'col'), may hold values from -0.125 to 0.125
- s_pattern: int32 [16, 16], replicated, may hold values 0 or 1
- h_pattern: int32 [16, 16], replicated, may hold values 0 or 1
- keep_mask: int32 [16, 16], replicated, may hold values 0 or 1
Outputs:
- z_next: float32 [4096, 4096], P('row', 'col')
- h_times_z: float32 [4096, 4096], P('row', 'col')
All inputs are finite; a program needn't handle non-finite values.
Results may differ from a plain program's by a relative error of at most 0.00013.
Values sent between devices are 32-bit elements; how exact they have to be, the bound alone decides.
No kernel may reach another device: no remote copies, remote signals or barrier semaphores. Data moves between devices by JAX's collectives and lax.ppermute only.
A program may use at most 128 MiB of HBM per device.

v0:
```python
import jax
import jax.numpy as jnp
from jax import lax
from jax.sharding import PartitionSpec as P

BLK = 256


def from_root(array, axis, root):
    mine = lax.axis_index(axis) == root
    return lax.psum(jnp.where(mine, array, jnp.zeros_like(array)), axis)


def expand(pattern):
    values = pattern.astype(jnp.float32)
    return jnp.repeat(jnp.repeat(values, BLK, axis=0), BLK, axis=1)


def product(left, right):
    return jnp.dot(left, right, preferred_element_type=jnp.float32, precision=lax.Precision.HIGHEST)


def local(y_blocks, z_blocks, h_blocks, s_pattern, h_pattern, keep_mask):
    nblocks = s_pattern.shape[0]
    row_blocks = y_blocks.shape[0] // BLK
    col_blocks = y_blocks.shape[1] // BLK
    row_at = lax.axis_index("row")
    col_at = lax.axis_index("col")
    layer_at = lax.axis_index("depth")

    def local_tile(pattern):
        return expand(
            lax.dynamic_slice(
                pattern, (row_at * row_blocks, col_at * col_blocks), (row_blocks, col_blocks)
            )
        )

    s_local = local_tile(s_pattern)
    keep_local = local_tile(keep_mask)
    masked_y = y_blocks * s_local
    masked_z = z_blocks * s_local
    masked_h = h_blocks * local_tile(h_pattern)

    def multiply(left, right):
        layers = lax.axis_size("depth")
        inner = nblocks // layers
        lowest = layer_at * inner
        step_width = min(inner, col_blocks, row_blocks)
        inner_at = lowest + 0
        piece_a = lax.dynamic_slice_in_dim(left, inner_at % col_blocks * BLK, step_width * BLK, 1)
        part_a = from_root(piece_a, "col", inner_at // col_blocks)
        part_b = from_root(right, "row", inner_at // row_blocks)
        summed = product(part_a, part_b)
        return summed

    def filter_part(values, row_offset, col_offset):
        keep_part = lax.dynamic_slice(keep_local, (row_offset, col_offset), values.shape)
        return keep_part * values

    def shift_part(values, row_offset, col_offset):
        filtered = filter_part(values, row_offset, col_offset)
        global_rows = (
            row_at * (row_blocks * BLK) + row_offset + jnp.arange(values.shape[0], dtype=jnp.int32)
        )
        global_cols = (
            col_at * (col_blocks * BLK) + col_offset + jnp.arange(values.shape[1], dtype=jnp.int32)
        )
        diagonal_ones = global_rows[:, None] == global_cols[None, :]
        return jnp.where(diagonal_ones, 1.5, 0.0).astype(jnp.float32) - 0.5 * filtered

    def combine_depth(partial_sum, finish):
        share = lax.psum_scatter(partial_sum, "depth", scatter_dimension=0, tiled=True)
        finished = finish(share, layer_at * share.shape[0], 0)
        return lax.all_gather(finished, "depth", axis=0, tiled=True)

    q_matrix = combine_depth(multiply(masked_z, masked_y), shift_part)
    z_next = combine_depth(multiply(q_matrix, masked_z), filter_part)
    h_times_z = combine_depth(multiply(masked_h, z_next), filter_part)
    return (z_next, h_times_z)


def solution(mesh):
    in_specs = (P("row", "col"), P("row", "col"), P("row", "col"), P(), P(), P())
    out_specs = (P("row", "col"), P("row", "col"))
    return jax.shard_map(local, mesh=mesh, in_specs=in_specs, out_specs=out_specs, check_vma=False)
```

profile of v0, /device:TPU:24, one launch (start us, length us, event | category | flops | bytes accessed | tf_op | source)
XLA Modules:
  0.0 970.4 jit_solution(15851494755314473935)
XLA Ops:
  8.1 5.1 broadcast_select_fusion.1
  14.7 38.4 %all-reduce.7.cloned.1.call-done = f32[256,256]{1,0:T(8,128)} async-done(((f32[256,256]{1,0:T(8,128)}), f32[256,256]{1,0:T(8,128)}) %all-reduce.7.cloned.1.call-update) | async-done | bytes 262160 | tf_op jit(solution)/shard_map/psum | solution.py:11
  53.1 217.4 %all-reduce.11.cloned.1.call-done = (f32[256,2048]{1,0:T(8,128)}, f32[256,2048]{1,0:T(8,128)}) async-done(((f32[256,2048]{1,0:T(8,128)}, f32[256,2048]{1,0:T(8,128)}), (f32[256,2048]{1,0:T(8,128)}, f32[256,2048]{1,0:T(8,128)})) %all-reduce.11.cloned.1.call-update) | async-done | bytes 4194320 | tf_op jit(solution)/shard_map/psum | solution.py:11
  270.5 4.9 fusion.1
  275.5 0.9 convert_bitcast_fusion
  276.5 77.8 %reduce-scatter.4.cloned.1.call-done = f32[16,2048]{1,0:T(8,128)} async-done(((f32[256,2048]{1,0:T(8,128)}), f32[16,2048]{1,0:T(8,128)}) %reduce-scatter.4.cloned.1.call-update) | async-done | bytes 131088 | tf_op jit(solution)/shard_map/reduce_scatter | solution.py:72
  354.3 1.6 multiply_subtract_fusion
  356.2 1.7 fusion
  357.8 73.7 %all-gather.4.cloned.1.call-done = f32[256,2048]{1,0:T(8,128)} async-done(((f32[16,2048]{1,0:T(8,128)}), f32[256,2048]{1,0:T(8,128)}) %all-gather.4.cloned.1.call-update) | async-done | bytes 2097168 | tf_op jit(solution)/shard_map/all_gather | solution.py:74
  431.5 1.7 dynamic-slice_select_fusion
  433.3 34.2 %all-reduce.13.cloned.1.call-done = (f32[256,256]{1,0:T(8,128)}, f32[256,256]{1,0:T(8,128)}) async-done(((f32[256,256]{1,0:T(8,128)}, f32[256,256]{1,0:T(8,128)}), (f32[256,256]{1,0:T(8,128)}, f32[256,256]{1,0:T(8,128)})) %all-reduce.13.cloned.1.call-update) | async-done | bytes 524304 | tf_op jit(solution)/shard_map/psum | solution.py:11
  467.5 4.2 fusion.2
  471.8 80.1 %reduce-scatter.6.cloned.1.call-done = f32[16,2048]{1,0:T(8,128)} async-done(((f32[256,2048]{1,0:T(8,128)}), f32[16,2048]{1,0:T(8,128)}) %reduce-scatter.6.cloned.1.call-update) | async-done | bytes 131088 | tf_op jit(solution)/shard_map/reduce_scatter | solution.py:72
  551.9 1.6 broadcast_multiply_fusion.2
  553.5 75.4 %all-gather.6.cloned.1.call-done = f32[256,2048]{1,0:T(8,128)} async-done(((f32[16,2048]{1,0:T(8,128)}), f32[256,2048]{1,0:T(8,128)}) %all-gather.6.cloned.1.call-update) | async-done | bytes 2097168 | tf_op jit(solution)/shard_map/all_gather | solution.py:74
  628.9 1.5 broadcast_select_fusion
  630.5 170.2 %all-reduce.9.cloned.1.call-done = f32[256,2048]{1,0:T(8,128)} async-done(((f32[256,2048]{1,0:T(8,128)}), f32[256,2048]{1,0:T(8,128)}) %all-reduce.9.cloned.1.call-update) | async-done | bytes 2097168 | tf_op jit(solution)/shard_map/psum | solution.py:11
  800.7 4.8 fusion.3
  805.5 77.8 %reduce-scatter.8.cloned.1.call-done = f32[16,2048]{1,0:T(8,128)} async-done(((f32[256,2048]{1,0:T(8,128)}), f32[16,2048]{1,0:T(8,128)}) %reduce-scatter.8.cloned.1.call-update) | async-done | bytes 131088 | tf_op jit(solution)/shard_map/reduce_scatter | solution.py:72
  883.3 1.6 broadcast_multiply_fusion.1
  884.9 75.0 %all-gather.8.cloned.1.call-done = f32[256,2048]{1,0:T(8,128)} async-done(((f32[16,2048]{1,0:T(8,128)}), f32[256,2048]{1,0:T(8,128)}) %all-gather.8.cloned.1.call-update) | async-done | bytes 2097168 | tf_op jit(solution)/shard_map/all_gather | solution.py:74
  959.9 1.3 copy.19
  961.2 1.0 copy-done.2
  962.3 1.3 copy.20
  (38 shorter events, 3.1 us)
Async XLA Ops:
  7.2 45.9 %all-reduce.7.cloned.1.call-start = ((), (), s32[]{:S(2)}) async-start(), calls=%async_computation.3 | async-start | bytes 524288 | tf_op jit(solution)/shard_map/psum | solution.py:11
  13.9 256.6 %all-reduce.11.cloned.1.call-start = ((), (), s32[]{:S(2)}) async-start(), calls=%async_computation.11 | async-start | bytes 8388608 | tf_op jit(solution)/shard_map/psum | solution.py:11
  14.7 339.6 %reduce-scatter.4.cloned.1.call-start = ((), (), s32[]{:S(2)}) async-start(), calls=%async_computation.4 | async-start | bytes 2228224 | tf_op jit(solution)/shard_map/reduce_scatter | solution.py:72
  275.4 192.1 %copy-start.1 = (f32[256,2048]{1,0:T(8,128)S(1)}, f32[256,2048]{1,0:T(8,128)}, u32[]{:S(2)}) copy-start(f32[256,2048]{1,0:T(8,128)} %get-tuple-element.3) | copy-start | bytes 6291460
  275.4 156.1 %all-gather.4.cloned.1.call-start = ((), (), s32[]{:S(2)}) async-start(), calls=%async_computation.5 | async-start | bytes 2228224 | tf_op jit(solution)/shard_map/all_gather | solution.py:74
  356.0 111.5 %all-reduce.13.cloned.1.call-start = ((), (), s32[]{:S(2)}) async-start(), calls=%async_computation.12 | async-start | bytes 1048576 | tf_op jit(solution)/shard_map/psum | solution.py:11
  433.2 118.6 %reduce-scatter.6.cloned.1.call-start = ((), (), s32[]{:S(2)}) async-start(), calls=%async_computation.6 | async-start | bytes 2228224 | tf_op jit(solution)/shard_map/reduce_scatter | solution.py:72
  471.7 157.2 %all-gather.6.cloned.1.call-start = ((), (), s32[]{:S(2)}) async-start(), calls=%async_computation.7 | async-start | bytes 2228224 | tf_op jit(solution)/shard_map/all_gather | solution.py:74
  553.5 247.2 %all-reduce.9.cloned.1.call-start = ((), (), s32[]{:S(2)}) async-start(), calls=%async_computation.8 | async-start | bytes 4194304 | tf_op jit(solution)/shard_map/psum | solution.py:11
  630.5 170.2 %copy-start.3 = (f32[256,256]{1,0:T(8,128)S(1)}, f32[256,256]{1,0:T(8,128)}, u32[]{:S(2)}) copy-start(f32[256,256]{1,0:T(8,128)} %get-tuple-element.5) | copy-start | bytes 786436
  630.5 252.9 %reduce-scatter.8.cloned.1.call-start = ((), (), s32[]{:S(2)}) async-start(), calls=%async_computation.9 | async-start | bytes 2228224 | tf_op jit(solution)/shard_map/reduce_scatter | solution.py:72
  805.5 154.4 %copy-start = (f32[256,2048]{1,0:T(8,128)S(1)}, f32[256,2048]{1,0:T(8,128)}, u32[]{:S(2)}) copy-start(f32[256,2048]{1,0:T(8,128)} %all-gather.6.cloned.1.call-done) | copy-start | bytes 6291460
  805.5 154.4 %all-gather.8.cloned.1.call-start = ((), (), s32[]{:S(2)}) async-start(), calls=%async_computation.10 | async-start | bytes 2228224 | tf_op jit(solution)/shard_map/all_gather | solution.py:74
  959.9 2.3 copy-start.2
Sparse Core Ops, SparseCore 0:
  14.0 39.0 all-reduce.6
  57.0 213.5 all-reduce.10
  275.6 78.6 reduce-scatter.3
  357.0 74.4 all-gather.3
  435.1 32.3 all-reduce.12
  471.8 79.9 reduce-scatter.5
  554.5 74.3 all-gather.5
  632.4 168.2 all-reduce.8
  805.6 77.6 reduce-scatter.7
  885.8 74.0 all-gather.7
where the time goes:
time: 971 us; the launch traced here: 970 us
  waiting for transfers between devices  921 us (95%)
  other arithmetic  17.1 us (2%)
  between operations  14.2 us (1%)
  matrix products  13.9 us (1%)
    psum x4, waiting for transfers between devices, from_root(): return lax.psum(jnp.where(mine, array, jnp.zeros_like(array)), axis)  460 us
    reduce_scatter x3, waiting for transfers between devices, combine_depth(): lax.psum_scatter(partial_sum, 'depth', scatter_dimension=0, tiled=True)  236 us
    all_gather x3, waiting for transfers between devices, combine_depth(): return lax.all_gather(finished, 'depth', axis=0, tiled=True)  224 us
  transfers between devices with their start and end apart: 10, of which 10 were waited for; matrix products, arithmetic and copies ran while one was open for 0% of the time, Pallas kernels for 0%

commit v1 on v0

--- a/solution.py
+++ b/solution.py
@@ -6,9 +6,13 @@
 BLK = 256
 
 
+def begin_ways_by_axis(point, named_axis):
+    return jnp.sum(lax.all_gather(point, axis_name=named_axis), axis=0)
+
+
 def from_root(array, axis, root):
     mine = lax.axis_index(axis) == root
-    return lax.psum(jnp.where(mine, array, jnp.zeros_like(array)), axis)
+    return begin_ways_by_axis(jnp.where(mine, array, jnp.zeros_like(array)), axis)
 
 
 def expand(pattern):

time: 971 us -> 1780 us (1.83)
  waiting for transfers between devices: 921 us -> 1690 us
  other arithmetic: 17.1 us -> 51.4 us
    all_gather x0 -> x3, waiting for transfers between devices: none -> 1250 us  [begin_ways_by_axis(): return jnp.sum(lax.all_gather(point, axis_name=named_axis), axis=0)]
    psum x4 -> x0, waiting for transfers between devices: 460 us -> none  [from_root(): return lax.psum(jnp.where(mine, array, jnp.zeros_like(array)), axis)]
    reduce_sum x0 -> x6, other arithmetic: none -> 35.5 us  [begin_ways_by_axis(): return jnp.sum(lax.all_gather(point, axis_name=named_axis), axis=0)]
  transfers between devices with their start and end apart: 10 -> 9, of which waited for: 10 -> 9; matrix products, arithmetic and copies ran while one was open for 0% -> 1% of each run, Pallas kernels for 0% -> 0%
where the time goes in v1:
time: 1780 us
  waiting for transfers between devices  1690 us (95%)
  other arithmetic  51.4 us (3%)
    all_gather x3, waiting for transfers between devices, begin_ways_by_axis(): return jnp.sum(lax.all_gather(point, axis_name=named_axis), axis=0)  1250 us
    reduce_scatter x3, waiting for transfers between devices, combine_depth(): lax.psum_scatter(partial_sum, 'depth', scatter_dimension=0, tiled=True)  227 us
    all_gather x3, waiting for transfers between devices, combine_depth(): return lax.all_gather(finished, 'depth', axis=0, tiled=True)  215 us
  transfers between devices with their start and end apart: 9, of which 9 were waited for; matrix products, arithmetic and copies ran while one was open for 1% of the time, Pallas kernels for 0%

profile of v1, /device:TPU:24, one launch (start us, length us, event | category | flops | bytes accessed | tf_op | source)
XLA Modules:
  0.0 1779.9 jit_solution(9365834841171555758)
XLA Ops:
  8.1 5.2 broadcast_select_fusion.1
  13.4 2.2 all-gather
  15.6 420.2 %all-gather.19.cloned.1.call-done = f32[4096,2048]{1,0:T(8,128)} async-done(((f32[256,2048]{1,0:T(8,128)}), f32[4096,2048]{1,0:T(8,128)}) %all-gather.19.cloned.1.call-update) | async-done | bytes 33554448 | tf_op jit(solution)/shard_map/all_gather | solution.py:10
  435.9 11.8 reduce_sum.55
  447.7 3.2 fusion.1
  452.6 74.5 %reduce-scatter.4.cloned.1.call-done = f32[16,2048]{1,0:T(8,128)} async-done(((f32[256,2048]{1,0:T(8,128)}), f32[16,2048]{1,0:T(8,128)}) %reduce-scatter.4.cloned.1.call-update) | async-done | bytes 131088 | tf_op jit(solution)/shard_map/reduce_scatter | solution.py:76
  527.1 1.6 multiply_subtract_fusion
  528.8 418.0 %all-gather.21.cloned.1.call-done = f32[4096,2048]{1,0:T(8,128)} async-done(((f32[256,2048]{1,0:T(8,128)}), f32[4096,2048]{1,0:T(8,128)}) %all-gather.21.cloned.1.call-update) | async-done | bytes 33554448 | tf_op jit(solution)/shard_map/all_gather | solution.py:10
  946.8 11.8 reduce_sum.57
  958.6 64.3 %all-gather.13.cloned.1.call-done = f32[256,2048]{1,0:T(8,128)} async-done(((f32[16,2048]{1,0:T(8,128)}), f32[256,2048]{1,0:T(8,128)}) %all-gather.13.cloned.1.call-update) | async-done | bytes 2097168 | tf_op jit(solution)/shard_map/all_gather | solution.py:78
  1023.9 2.2 all-gather.2
  1026.1 3.2 fusion.2
  1029.4 76.1 %reduce-scatter.6.cloned.1.call-done = f32[16,2048]{1,0:T(8,128)} async-done(((f32[256,2048]{1,0:T(8,128)}), f32[16,2048]{1,0:T(8,128)}) %reduce-scatter.6.cloned.1.call-update) | async-done | bytes 131088 | tf_op jit(solution)/shard_map/reduce_scatter | solution.py:76
  1105.4 1.6 broadcast_multiply_fusion.2
  1107.1 75.4 %all-gather.15.cloned.1.call-done = f32[256,2048]{1,0:T(8,128)} async-done(((f32[16,2048]{1,0:T(8,128)}), f32[256,2048]{1,0:T(8,128)}) %all-gather.15.cloned.1.call-update) | async-done | bytes 2097168 | tf_op jit(solution)/shard_map/all_gather | solution.py:78
  1182.5 1.5 broadcast_select_fusion
  1186.0 2.2 all-gather.4
  1188.3 413.2 %all-gather.23.cloned.1.call-done = f32[4096,2048]{1,0:T(8,128)} async-done(((f32[256,2048]{1,0:T(8,128)}), f32[4096,2048]{1,0:T(8,128)}) %all-gather.23.cloned.1.call-update) | async-done | bytes 33554448 | tf_op jit(solution)/shard_map/all_gather | solution.py:10
  1601.4 11.8 reduce_sum.59
  1613.3 3.2 fusion.3
  1616.6 76.3 %reduce-scatter.8.cloned.1.call-done = f32[16,2048]{1,0:T(8,128)} async-done(((f32[256,2048]{1,0:T(8,128)}), f32[16,2048]{1,0:T(8,128)}) %reduce-scatter.8.cloned.1.call-update) | async-done | bytes 131088 | tf_op jit(solution)/shard_map/reduce_scatter | solution.py:76
  1692.8 1.6 broadcast_multiply_fusion.1
  1694.4 75.3 %all-gather.17.cloned.1.call-done = f32[256,2048]{1,0:T(8,128)} async-done(((f32[16,2048]{1,0:T(8,128)}), f32[256,2048]{1,0:T(8,128)}) %all-gather.17.cloned.1.call-update) | async-done | bytes 2097168 | tf_op jit(solution)/shard_map/all_gather | solution.py:78
  1769.7 1.3 copy.13
  (41 shorter events, 8.2 us)
Async XLA Ops:
  7.2 428.7 %all-gather.19.cloned.1.call-start = ((), (), s32[]{:S(2)}) async-start(), calls=%async_computation.9 | async-start | bytes 35651584 | tf_op jit(solution)/shard_map/all_gather | solution.py:10
  13.3 513.8 %reduce-scatter.4.cloned.1.call-start = ((), (), s32[]{:S(2)}) async-start(), calls=%async_computation.3 | async-start | bytes 2228224 | tf_op jit(solution)/shard_map/reduce_scatter | solution.py:76
  450.9 495.8 %all-gather.21.cloned.1.call-start = ((), (), s32[]{:S(2)}) async-start(), calls=%async_computation.10 | async-start | bytes 35651584 | tf_op jit(solution)/shard_map/all_gather | solution.py:10
  451.7 571.2 %all-gather.13.cloned.1.call-start = ((), (), s32[]{:S(2)}) async-start(), calls=%async_computation.4 | async-start | bytes 2228224 | tf_op jit(solution)/shard_map/all_gather | solution.py:78
  528.8 576.7 %reduce-scatter.6.cloned.1.call-start = ((), (), s32[]{:S(2)}) async-start(), calls=%async_computation.5 | async-start | bytes 2228224 | tf_op jit(solution)/shard_map/reduce_scatter | solution.py:76
  1029.3 153.2 %all-gather.15.cloned.1.call-start = ((), (), s32[]{:S(2)}) async-start(), calls=%async_computation.6 | async-start | bytes 2228224 | tf_op jit(solution)/shard_map/all_gather | solution.py:78
  1107.0 494.4 %all-gather.23.cloned.1.call-start = ((), (), s32[]{:S(2)}) async-start(), calls=%async_computation.11 | async-start | bytes 35651584 | tf_op jit(solution)/shard_map/all_gather | solution.py:10
  1184.1 508.7 %reduce-scatter.8.cloned.1.call-start = ((), (), s32[]{:S(2)}) async-start(), calls=%async_computation.7 | async-start | bytes 2228224 | tf_op jit(solution)/shard_map/reduce_scatter | solution.py:76
  1616.5 153.2 %copy-start = (f32[256,2048]{1,0:T(8,128)S(1)}, f32[256,2048]{1,0:T(8,128)}, u32[]{:S(2)}) copy-start(f32[256,2048]{1,0:T(8,128)} %all-gather.15.cloned.1.call-done) | copy-start | bytes 6291460
  1616.5 153.2 %all-gather.17.cloned.1.call-start = ((), (), s32[]{:S(2)}) async-start(), calls=%async_computation.8 | async-start | bytes 2228224 | tf_op jit(solution)/shard_map/all_gather | solution.py:78
  1769.7 2.3 copy-start.1
Sparse Core Ops, SparseCore 0:
  13.4 422.3 all-gather.18
  451.1 75.9 reduce-scatter.3
  530.9 415.8 all-gather.20
  949.3 73.5 all-gather.12
  1029.4 75.9 reduce-scatter.5
  1107.9 74.5 all-gather.14
  1186.3 415.1 all-gather.22
  1616.6 76.1 reduce-scatter.7
  1695.5 74.1 all-gather.16
